TPU v7x, 128 devices: a whole 4x4x4 slice. The times are simulated.
128 devices in a mesh: dp: 16 (over z, x), expert: 8 (over y, core).
Axes of the slice: x: 4, y: 4, z: 4, core: 2. Of those that a mesh axis runs over, the one named last changes fastest.
Arguments:
- local_grads: bfloat16 [16, 8, 4, 1048576], P('dp', 'expert')
- master_weights: float32 [8, 4, 1048576], P('expert', None, 'dp'), may hold values from -6 to 6
- first_moment: float32 [8, 4, 1048576], P('expert', None, 'dp')
- second_moment: float32 [8, 4, 1048576], P('expert', None, 'dp')
Outputs:
- new_params: bfloat16 [8, 4, 1048576], P('expert')
- new_master: float32 [8, 4, 1048576], P('expert', None, 'dp')
- new_first: float32 [8, 4, 1048576], P('expert', None, 'dp')
- new_second: float32 [8, 4, 1048576], P('expert', None, 'dp')
All inputs are finite; a program needn't handle non-finite values.
Results may differ from a plain program's by a relative error of at most 0.0013.
Values may be sent and summed in bfloat16 or wider, within the bound.
No kernel may reach another device: no remote copies, remote signals or barrier semaphores. Data moves between devices by JAX's collectives and lax.ppermute only.
A program may use at most 128 MiB of HBM per device.

v0:
```python
import functools
import jax
import jax.numpy as jnp
from jax import lax
from jax.sharding import Mesh
from jax.sharding import PartitionSpec as P

DP = ("dp_0", "dp_1")
DP_EXPERT = ("dp_0", "dp_1", "expert_0", "expert_1")
EXPERT = ("expert_0", "expert_1")
beta_first = 0.9
beta_second = 0.95
correct_first = 1.0 - 0.9**10
correct_second = 1.0 - 0.95**10
learn_rate = 0.05
decay_rate = 0.1
clip_limit = 1.0
tiny_eps = 1e-08
norm_eps = 1e-06


def by_axis(x, axes):
    return functools.reduce(lax.psum, axes, x)


def adam_update(gradient, master, first, second, clip_factor):
    scaled = clip_factor * gradient
    new_first = beta_first * first + (1.0 - beta_first) * scaled
    new_second = beta_second * second + (1.0 - beta_second) * scaled * scaled
    direction = new_first / correct_first / (jnp.sqrt(new_second / correct_second) + tiny_eps)
    new_master = master - learn_rate * (decay_rate * master + direction)
    return (new_master, new_first, new_second)


def shards(local_grads, master_weights, first_moment, second_moment):
    replicas = lax.axis_size(DP)
    own_grads = local_grads[0, 0]
    layer_count = own_grads.shape[0]
    share = own_grads.shape[1] // replicas
    pieces_all = own_grads.reshape(layer_count, replicas, share)
    arrived = lax.all_to_all(pieces_all, DP, split_axis=1, concat_axis=1, tiled=True)
    reduced = jnp.sum(arrived.astype(jnp.float32), axis=1)
    mean_grad = reduced / replicas
    squares = jnp.sum(mean_grad * mean_grad)
    total_squares = by_axis(squares, DP_EXPERT)
    grad_norm = jnp.sqrt(total_squares)
    clip_factor = jnp.minimum(1.0, clip_limit / (grad_norm + norm_eps))
    new_master, new_first, new_second = adam_update(
        mean_grad, master_weights[0], first_moment[0], second_moment[0], clip_factor
    )
    rounded = new_master.astype(jnp.bfloat16)
    gathered = lax.all_gather(rounded, DP, axis=1, tiled=True)
    return (gathered[None], new_master[None], new_first[None], new_second[None])


def solution(mesh):
    torus = Mesh(mesh.devices.reshape(4, 4, 4, 2), ("dp_0", "dp_1", "expert_0", "expert_1"))
    return jax.shard_map(
        shards,
        mesh=torus,
        in_specs=(
            P(DP, EXPERT, None, None),
            P(EXPERT, None, DP),
            P(EXPERT, None, DP),
            P(EXPERT, None, DP),
        ),
        out_specs=(
            P(EXPERT, None, None),
            P(EXPERT, None, DP),
            P(EXPERT, None, DP),
            P(EXPERT, None, DP),
        ),
        check_vma=False,
    )
```

profile of v0, /device:TPU:1, one launch (start us, length us, event | category | flops | bytes accessed | tf_op | source)
XLA Modules:
  0.0 238.8 jit_solution(16362549095326047776)
XLA Ops:
  7.2 0.0 all-gather.2.cloned.1.call-start
  7.2 103.3 %all_to_all.5 = bf16[4,16,65536]{2,0,1:T(4,128)(2,1)} all-to-all(bf16[4,16,65536]{2,0,1:T(4,128)(2,1)} %bitcast.32), channel_id=1, replica_groups=mesh['dp_0'=4,'dp_1'=4,'expert_0'=4,'expert_1'=2] {'dp_0','dp_1'}, dimensions={1} | all-to-all | bytes 16777216 | tf_op jit(solution)/shard_map/all_to_all | solution.py:41
  110.5 0.0 copy-start
  110.5 0.0 copy-start.1
  110.5 7.2 %convert_reduce_fusion = f32[4,65536]{1,0:T(4,128)S(1)} fusion(bf16[4,16,65536]{2,0,1:T(4,128)(2,1)} %all_to_all.5), kind=kLoop, calls=%fused_computation | loop fusion | flops 8126464 | bytes 9437184 | tf_op jit(solution)/shard_map/reduce_sum | solution.py:42
  117.8 1.1 multiply_reduce_fusion
  118.9 7.3 %psum.28 = f32[]{:T(128)} all-reduce(f32[]{:T(128)} %multiply_reduce_fusion), channel_id=1, replica_groups=mesh['dp_0'=4,'dp_1'=4,'expert_0'=4,'expert_1'=2] {'dp_0'}, use_global_device_ids=true, to_apply=%region_2.0 | all-reduce | flops 1 | bytes 8 | tf_op jit(solution)/shard_map/psum | solution.py:23
  126.3 7.2 %psum.29 = f32[]{:T(128)} all-reduce(f32[]{:T(128)} %psum.28), channel_id=1, replica_groups=mesh['dp_0'=4,'dp_1'=4,'expert_0'=4,'expert_1'=2] {'dp_1'}, use_global_device_ids=true, to_apply=%region_3.0 | all-reduce | flops 1 | bytes 8 | tf_op jit(solution)/shard_map/psum | solution.py:23
  133.4 9.3 %psum.30 = f32[]{:T(128)} all-reduce(f32[]{:T(128)} %psum.29), channel_id=1, replica_groups=mesh['dp_0'=4,'dp_1'=4,'expert_0'=4,'expert_1'=2] {'expert_0'}, use_global_device_ids=true, to_apply=%region_4.0 | all-reduce | flops 1 | bytes 8 | tf_op jit(solution)/shard_map/psum | solution.py:23
  142.8 10.6 %psum.31 = f32[]{:T(128)} all-reduce(f32[]{:T(128)} %psum.30), channel_id=1, replica_groups=mesh['dp_0'=4,'dp_1'=4,'expert_0'=4,'expert_1'=2] {'expert_1'}, use_global_device_ids=true, to_apply=%region_5.0 | all-reduce | flops 1 | bytes 8 | tf_op jit(solution)/shard_map/psum | solution.py:23
  154.1 0.0 copy-done
  154.1 0.0 copy-done.1
  154.1 3.7 %fusion.10 = bf16[4,65536]{1,0:T(4,128)(2,1)} fusion(f32[1,4,65536]{2,1,0:T(4,128)S(1)} %copy-done, f32[1,4,65536]{2,1,0:T(4,128)S(1)} %copy-done.1, f32[1,4,65536]{2,1,0:T(4,128)} %param.6, f32[4,65536]{1,0:T(4,128)S(1)} %convert_reduce_fusion, f32[]{:T(128)S(6)} %mul.104), kind=kLoop, calls=%fused_computation.17 | loop fusion | flops 4456448 | bytes 4718596 | tf_op jit(solution)/shard_map/convert_element_type | solution.py:51
  157.9 0.0 all-gather.2.cloned.1.call-update
  157.9 4.5 %multiply_subtract_fusion = (f32[1,4,65536]{2,1,0:T(4,128)}, f32[1,4,65536]{2,1,0:T(4,128)}, f32[1,4,65536]{2,1,0:T(4,128)}) fusion(f32[1,4,65536]{2,1,0:T(4,128)S(1)} %copy-done, f32[4,65536]{1,0:T(4,128)S(1)} %convert_reduce_fusion, f32[]{:T(128)S(6)} %mul.104, f32[1,4,65536]{2,1,0:T(4,128)} %param.6, f32[1,4,65536]{2,1,0:T(4,128)S(1)} %copy-done.1), kind=kLoop, calls=%fused_computation.18 | loop fusion | flops 4194304 | bytes 7340036 | tf_op jit(solution)/shard_map/sub | solution.py:31
  162.3 61.5 %all-gather.2.cloned.1.call-done = bf16[4,1048576]{1,0:T(4,128)(2,1)} async-done(((bf16[4,65536]{1,0:T(4,128)(2,1)}), bf16[4,1048576]{1,0:T(4,128)(2,1)}) %all-gather.2.cloned.1.call-update) | async-done | bytes 8388624 | tf_op jit(solution)/shard_map/all_gather | solution.py:52
  223.9 8.1 %copy.9 = bf16[1,4,1048576]{2,1,0:T(4,128)(2,1)} copy(bf16[1,4,1048576]{2,1,0:T(4,128)(2,1)} %bitcast.33) | data formatting | bytes 16777216
Async XLA Ops:
  7.2 216.7 %all-gather.2.cloned.1.call-start = ((), (), s32[]{:S(2)}) async-start(), calls=%async_computation.1 | async-start | bytes 8912896 | tf_op jit(solution)/shard_map/all_gather | solution.py:52
  110.5 43.6 %copy-start = (f32[1,4,65536]{2,1,0:T(4,128)S(1)}, f32[1,4,65536]{2,1,0:T(4,128)}, u32[]{:S(2)}) copy-start(f32[1,4,65536]{2,1,0:T(4,128)} %param.5) | copy-start | bytes 3145732
  110.5 43.6 %copy-start.1 = (f32[1,4,65536]{2,1,0:T(4,128)S(1)}, f32[1,4,65536]{2,1,0:T(4,128)}, u32[]{:S(2)}) copy-start(f32[1,4,65536]{2,1,0:T(4,128)} %param.7) | copy-start | bytes 3145732
Sparse Core Ops, SparseCore 0:
  158.0 65.8 all-gather.1
where the time goes:
time: 239 us
  blocking collectives  138 us (58%)
  waiting for transfers between devices  61.5 us (26%)
  other arithmetic  16.6 us (7%)
  between operations  14.8 us (6%)
  local copies, waits for them, and re-layouts  8.06 us (3%)
    all_to_all x1, blocking collectives, shards(): lax.all_to_all(pieces_all, DP, split_axis=1, concat_axis=1, tiled=True)  103 us
    all_gather x1, waiting for transfers between devices, shards(): gathered = lax.all_gather(rounded, DP, axis=1, tiled=True)  61.5 us
    psum x4, blocking collectives, by_axis(): return functools.reduce(lax.psum, axes, x)  34.5 us
    unnamed x5, local copies, waits for them, and re-layouts  8.06 us
    reduce_sum x1, other arithmetic, shards(): reduced = jnp.sum(arrived.astype(jnp.float32), axis=1)  7.25 us
  transfers between devices with their start and end apart: 1, of which 1 were waited for; matrix products, arithmetic and copies ran while one was open for 2% of the time, Pallas kernels for 0%

commit v1 on v0

--- a/solution.py
+++ b/solution.py
@@ -49,7 +49,9 @@
         mean_grad, master_weights[0], first_moment[0], second_moment[0], clip_factor
     )
     rounded = new_master.astype(jnp.bfloat16)
-    gathered = lax.all_gather(rounded, DP, axis=1, tiled=True)
+    gathered = jnp.concatenate(
+        lax.all_to_all(jnp.stack([rounded] * lax.axis_size(DP)), DP, 0, 0), axis=1
+    )
     return (gathered[None], new_master[None], new_first[None], new_second[None])
 
 

time: 239 us -> 262 us (1.096)
  blocking collectives: 138 us -> 238 us
  waiting for transfers between devices: 61.5 us -> 0 us
  between operations: 14.8 us -> 1.38 us
  other arithmetic: 16.6 us -> 13.1 us
    all_to_all x0 -> x1, blocking collectives: none -> 99.8 us  [shards(): lax.all_to_all(jnp.stack([rounded] * lax.axis_size(DP)), DP, 0, 0)]
    all_gather x1 -> x0, waiting for transfers between devices: 61.5 us -> none  [shards(): gathered = lax.all_gather(rounded, DP, axis=1, tiled=True)]
    another operation x0 -> x1, local copies, waits for them, and re-layouts: none -> 6.63 us  [shards(): jnp.stack([rounded] * lax.axis_size(DP))]
    another operation x0 -> x1, other arithmetic: none -> 4.79 us  [shards(): jnp.stack([rounded] * lax.axis_size(DP))]
    unnamed x5 -> x3, local copies, waits for them, and re-layouts: 8.06 us -> 3.4 us
    sub x1 -> x0, other arithmetic: 4.45 us -> none  [adam_update(): new_master = master - learn_rate * (decay_rate * master + direction)]
    convert_element_type x1 -> x0, other arithmetic: 3.72 us -> none  [shards(): rounded = new_master.astype(jnp.bfloat16)]
  transfers between devices with their start and end apart: 1 -> 0, of which waited for: 1 -> 0; matrix products, arithmetic and copies ran while one was open for 2% -> 0% of each run, Pallas kernels for 0% -> 0%
where the time goes in v1:
time: 262 us
  blocking collectives  238 us (91%)
  other arithmetic  13.1 us (5%)
  local copies, waits for them, and re-layouts  10 us (4%)
    all_to_all x1, blocking collectives, shards(): lax.all_to_all(pieces_all, DP, split_axis=1, concat_axis=1, tiled=True)  103 us
    all_to_all x1, blocking collectives, shards(): lax.all_to_all(jnp.stack([rounded] * lax.axis_size(DP)), DP, 0, 0)  99.8 us
    psum x4, blocking collectives, by_axis(): return functools.reduce(lax.psum, axes, x)  34.5 us
    reduce_sum x1, other arithmetic, shards(): reduced = jnp.sum(arrived.astype(jnp.float32), axis=1)  7.19 us
    another operation x1, local copies, waits for them, and re-layouts, shards(): jnp.stack([rounded] * lax.axis_size(DP))  6.63 us

profile of v1, /device:TPU:1, one launch (start us, length us, event | category | flops | bytes accessed | tf_op | source)
XLA Modules:
  0.0 262.1 jit_solution(15066226098057949123)
XLA Ops:
  0.6 103.3 %all_to_all.10 = bf16[4,16,65536]{2,0,1:T(4,128)(2,1)} all-to-all(bf16[4,16,65536]{2,0,1:T(4,128)(2,1)} %bitcast.14), channel_id=1, replica_groups=mesh['dp_0'=4,'dp_1'=4,'expert_0'=4,'expert_1'=2] {'dp_0','dp_1'}, dimensions={1} | all-to-all | bytes 16777216 | tf_op jit(solution)/shard_map/all_to_all | solution.py:41
  103.9 0.0 copy-start
  104.0 7.2 %convert_reduce_fusion = f32[4,65536]{1,0:T(4,128)S(1)} fusion(bf16[4,16,65536]{2,0,1:T(4,128)(2,1)} %all_to_all.10), kind=kLoop, calls=%fused_computation | loop fusion | flops 8126464 | bytes 9437184 | tf_op jit(solution)/shard_map/reduce_sum | solution.py:42
  111.1 1.1 multiply_reduce_fusion
  112.3 7.3 %psum.28 = f32[]{:T(128)} all-reduce(f32[]{:T(128)} %multiply_reduce_fusion), channel_id=1, replica_groups=mesh['dp_0'=4,'dp_1'=4,'expert_0'=4,'expert_1'=2] {'dp_0'}, use_global_device_ids=true, to_apply=%region_2.0 | all-reduce | flops 1 | bytes 8 | tf_op jit(solution)/shard_map/psum | solution.py:23
  119.6 7.2 %psum.29 = f32[]{:T(128)} all-reduce(f32[]{:T(128)} %psum.28), channel_id=1, replica_groups=mesh['dp_0'=4,'dp_1'=4,'expert_0'=4,'expert_1'=2] {'dp_1'}, use_global_device_ids=true, to_apply=%region_3.0 | all-reduce | flops 1 | bytes 8 | tf_op jit(solution)/shard_map/psum | solution.py:23
  126.8 9.3 %psum.30 = f32[]{:T(128)} all-reduce(f32[]{:T(128)} %psum.29), channel_id=1, replica_groups=mesh['dp_0'=4,'dp_1'=4,'expert_0'=4,'expert_1'=2] {'expert_0'}, use_global_device_ids=true, to_apply=%region_4.0 | all-reduce | flops 1 | bytes 8 | tf_op jit(solution)/shard_map/psum | solution.py:23
  136.1 10.6 %psum.31 = f32[]{:T(128)} all-reduce(f32[]{:T(128)} %psum.30), channel_id=1, replica_groups=mesh['dp_0'=4,'dp_1'=4,'expert_0'=4,'expert_1'=2] {'expert_1'}, use_global_device_ids=true, to_apply=%region_5.0 | all-reduce | flops 1 | bytes 8 | tf_op jit(solution)/shard_map/psum | solution.py:23
  147.5 0.0 copy-done
  147.5 4.8 %convert_bitcast_fusion = (bf16[4,65536]{1,0:T(4,128)(2,1)S(1)}, f32[1,4,65536]{2,1,0:T(4,128)}, f32[1,4,65536]{2,1,0:T(4,128)}, f32[1,4,65536]{2,1,0:T(4,128)}) fusion(f32[1,4,65536]{2,1,0:T(4,128)S(1)} %copy-done, f32[4,65536]{1,0:T(4,128)S(1)} %convert_reduce_fusion, f32[]{:T(128)S(6)} %mul.95, f32[1,4,65536]{2,1,0:T(4,128)} %param.6, f32[1,4,65536]{2,1,0:T(4,128)} %param.7), kind=kLoop, calls=%fused_computation.7 | loop fusion | flops 4456448 | bytes 7864324 | tf_op jit(solution)/shard_map/stack | solution.py:53
  152.3 6.6 %stack.5 = bf16[16,4,65536]{2,1,0:T(4,128)(2,1)} broadcast(bf16[4,65536]{1,0:T(4,128)(2,1)S(1)} %get-tuple-element.4), dimensions={1,2} | broadcast | bytes 8912896 | tf_op jit(solution)/shard_map/stack | solution.py:53
  158.9 99.8 %all_to_all.11 = bf16[16,4,65536]{2,1,0:T(4,128)(2,1)S(1)} all-to-all(bf16[16,4,65536]{2,1,0:T(4,128)(2,1)} %stack.5), channel_id=1, replica_groups=mesh['dp_0'=4,'dp_1'=4,'expert_0'=4,'expert_1'=2] {'dp_0','dp_1'}, dimensions={0} | all-to-all | bytes 16777216 | tf_op jit(solution)/shard_map/all_to_all | solution.py:53
  258.7 3.4 %copy.9 = bf16[1,4,1048576]{2,1,0:T(4,128)(2,1)} copy(bf16[1,4,1048576]{2,1,0:T(4,128)(2,1)S(1)} %bitcast.13) | data formatting | bytes 16777216
Async XLA Ops:
  103.9 43.5 %copy-start = (f32[1,4,65536]{2,1,0:T(4,128)S(1)}, f32[1,4,65536]{2,1,0:T(4,128)}, u32[]{:S(2)}) copy-start(f32[1,4,65536]{2,1,0:T(4,128)} %param.5) | copy-start | bytes 3145732
